TPU v7x, 32 devices: a whole 2x2x4 slice. The times are simulated.
32 devices in a mesh: ctx: 8 (over z, x), ch: 4 (over y, core).
Axes of the slice: x: 2, y: 2, z: 4, core: 2. Of those that a mesh axis runs over, the one named last changes fastest.
Arguments:
- proj: bfloat16 [3, 1024, 4096], P(None, 'ctx', 'ch'), may hold values from -6 to 6
- short_filter: float32 [3, 3, 4096], P(None, None, 'ch'), may hold values from -3 to 3
- long_filter: bfloat16 [1024, 4096], P('ctx', 'ch'), may hold values from -6 to 6
- out_grad: bfloat16 [1024, 4096], P('ctx', 'ch'), may hold values from -24 to 24
- conv_out: bfloat16 [1024, 4096], P('ctx', 'ch'), may hold values from -6 to 6
Outputs:
- proj_grad: bfloat16 [3, 1024, 4096], P(None, 'ctx', 'ch')
- short_grad: float32 [3, 3, 4096], P(None, None, 'ch')
- filter_grad: float32 [1024, 4096], P('ctx', 'ch')
- grad_square: float32 [], replicated
All inputs are finite; a program needn't handle non-finite values.
Results may differ from a plain program's by a relative error of at most 0.012.
Values may be sent and summed in bfloat16 or wider, within the bound.
A program may use at most 192 MiB of HBM per device.

v0:
```python
import functools
import math

import jax
import jax.numpy as jnp
import ml_dtypes
import numpy as np
from jax import lax
from jax.experimental import pallas as pl
from jax.experimental.pallas import tpu as pltpu
from jax.sharding import PartitionSpec as P


def to_pairs(matrix, ctx_count):
    local_rows, local_channels = matrix.shape
    channel_width = local_channels // ctx_count
    shaped = matrix.reshape(local_rows // 2, 2, ctx_count, channel_width)
    return jnp.transpose(shaped, (0, 2, 1, 3)).reshape(
        local_rows // 2, ctx_count * 2 * channel_width
    )


def from_pairs(matrix, ctx_count):
    half_rows, joined = matrix.shape
    channel_width = joined // (2 * ctx_count)
    shaped = matrix.reshape(half_rows, ctx_count, 2, channel_width)
    return jnp.transpose(shaped, (0, 2, 1, 3)).reshape(half_rows * 2, ctx_count * channel_width)


def rows_down(matrix, count):
    if count == 0:
        return matrix
    filler = jnp.zeros((count, matrix.shape[1]), matrix.dtype)
    return jnp.concatenate([filler, matrix[:-count]], axis=0)


def rows_up(matrix, count):
    if count == 0:
        return matrix
    filler = jnp.zeros((count, matrix.shape[1]), matrix.dtype)
    return jnp.concatenate([matrix[count:], filler], axis=0)


def retard(matrix, offset, channel_width):
    quotient, remainder = divmod(offset, 2)
    result = rows_down(matrix, quotient)
    if remainder:
        rolled = jnp.roll(result, channel_width, axis=1)
        first_half = lax.broadcasted_iota(jnp.int32, (1, matrix.shape[1]), 1) < channel_width
        result = jnp.where(first_half, rows_down(rolled, 1), rolled)
    return result


def advance(matrix, offset, channel_width):
    quotient, remainder = divmod(offset, 2)
    result = rows_up(matrix, quotient)
    if remainder:
        rolled = jnp.roll(result, channel_width, axis=1)
        first_half = lax.broadcasted_iota(jnp.int32, (1, matrix.shape[1]), 1) < channel_width
        result = jnp.where(first_half, rolled, rows_up(rolled, 1))
    return result


def fourier_table(count, period):
    row_index = lax.broadcasted_iota(jnp.int32, (count, count), 0)
    col_index = lax.broadcasted_iota(jnp.int32, (count, count), 1)
    exponent = row_index * col_index % period
    angle = exponent.astype(jnp.float32) * (-2.0 * math.pi / period)
    return (jnp.cos(angle), jnp.sin(angle))


def angle_pair(exponent, period):
    angle = exponent.astype(jnp.float32) * (-2.0 * math.pi / period)
    return (jnp.cos(angle), jnp.sin(angle))


def contract(form, real_table, imag_table, real_part, imag_part):
    highest = lax.Precision.HIGHEST
    first = jnp.einsum(form, real_table, real_part, precision=highest) - jnp.einsum(
        form, imag_table, imag_part, precision=highest
    )
    second = jnp.einsum(form, real_table, imag_part, precision=highest) + jnp.einsum(
        form, imag_table, real_part, precision=highest
    )
    return (first, second)


def rotate(real_part, imag_part, cosine_part, sine_part):
    return (
        real_part * cosine_part - imag_part * sine_part,
        real_part * sine_part + imag_part * cosine_part,
    )


def build_tables(radix_a, radix_b, radix_c, channel_width):
    period = radix_a * radix_b * radix_c
    shape_ab = (radix_a, radix_b, 1, 1)
    digit_ka = lax.broadcasted_iota(jnp.int32, shape_ab, 0)
    digit_sb = lax.broadcasted_iota(jnp.int32, shape_ab, 1)
    turn_ab = angle_pair(radix_c * digit_sb * digit_ka % period, period)
    shape_abc = (radix_a, radix_b, radix_c, 1)
    lower_k = lax.broadcasted_iota(jnp.int32, shape_abc, 0)
    middle_k = lax.broadcasted_iota(jnp.int32, shape_abc, 1)
    digit_sc = lax.broadcasted_iota(jnp.int32, shape_abc, 2)
    turn_bc = angle_pair(digit_sc * (lower_k + radix_a * middle_k) % period, period)
    whole_k = lower_k + radix_a * middle_k + radix_a * radix_b * digit_sc
    half_cos, half_sin = angle_pair(whole_k, 2 * period)
    first_half = lax.broadcasted_iota(jnp.int32, (1, 1, 1, 2 * channel_width), 3) < channel_width
    turn_half = (jnp.where(first_half, 1.0, half_cos), jnp.where(first_half, 0.0, half_sin))
    sign_vector = jnp.where(first_half, 1.0, -1.0)
    return (
        fourier_table(radix_a, radix_a),
        fourier_table(radix_b, radix_b),
        fourier_table(radix_c, radix_c),
        turn_ab,
        turn_bc,
        turn_half,
        sign_vector,
    )


def butterfly(values, sign_vector, channel_width):
    return sign_vector * values + jnp.roll(values, channel_width, axis=3)


def forward(signal, tables, radix_a, radix_b, radix_c, channel_width):
    table_a, table_b, table_c, turn_ab, turn_bc, turn_half, sign_vector = tables
    half_a = radix_a // 2
    values = signal.astype(jnp.float32).reshape(half_a, radix_b, radix_c, 2 * channel_width)
    highest = lax.Precision.HIGHEST
    real_part = jnp.einsum("ka,abcz->kbcz", table_a[0][:, :half_a], values, precision=highest)
    imag_part = jnp.einsum("ka,abcz->kbcz", table_a[1][:, :half_a], values, precision=highest)
    real_part, imag_part = rotate(real_part, imag_part, turn_ab[0], turn_ab[1])
    real_part, imag_part = contract("kb,abcz->akcz", table_b[0], table_b[1], real_part, imag_part)
    real_part, imag_part = rotate(real_part, imag_part, turn_bc[0], turn_bc[1])
    real_part, imag_part = contract("kc,abcz->abkz", table_c[0], table_c[1], real_part, imag_part)
    real_part, imag_part = rotate(real_part, imag_part, turn_half[0], turn_half[1])
    return (
        butterfly(real_part, sign_vector, channel_width),
        butterfly(imag_part, sign_vector, channel_width),
    )


def inverse(real_part, imag_part, tables, radix_a, radix_b, radix_c, channel_width):
    table_a, table_b, table_c, turn_ab, turn_bc, turn_half, sign_vector = tables
    half_a = radix_a // 2
    real_part = butterfly(real_part, sign_vector, channel_width)
    imag_part = butterfly(imag_part, sign_vector, channel_width)
    real_part, imag_part = rotate(real_part, imag_part, turn_half[0], -turn_half[1])
    real_part, imag_part = contract("kc,abcz->abkz", table_c[0], -table_c[1], real_part, imag_part)
    real_part, imag_part = rotate(real_part, imag_part, turn_bc[0], -turn_bc[1])
    real_part, imag_part = contract("kb,abcz->akcz", table_b[0], -table_b[1], real_part, imag_part)
    real_part, imag_part = rotate(real_part, imag_part, turn_ab[0], -turn_ab[1])
    real_part, imag_part = contract(
        "ka,abcz->kbcz", table_a[0][:half_a, :], -table_a[1][:half_a, :], real_part, imag_part
    )
    half_rows = half_a * radix_b * radix_c
    return (
        real_part.reshape(half_rows, 2 * channel_width),
        imag_part.reshape(half_rows, 2 * channel_width),
    )


def spectral(filter_pairs, product_u, product_g, ctx_count, local_rows):
    channel_width = filter_pairs.shape[1] // 2
    radix_b = local_rows // 16
    radix_c = 16
    sequence_length = ctx_count * local_rows
    tables = build_tables(ctx_count, radix_b, radix_c, channel_width)
    filter_real, filter_imag = forward(
        filter_pairs, tables, ctx_count, radix_b, radix_c, channel_width
    )
    gated_real, gated_imag = forward(product_u, tables, ctx_count, radix_b, radix_c, channel_width)
    grad_real, grad_imag = forward(product_g, tables, ctx_count, radix_b, radix_c, channel_width)
    input_real = filter_real * grad_real + filter_imag * grad_imag
    input_imag = filter_real * grad_imag - filter_imag * grad_real
    lag_real = gated_real * grad_real + gated_imag * grad_imag
    lag_imag = gated_real * grad_imag - gated_imag * grad_real
    joint_real, joint_imag = inverse(
        input_real - lag_imag,
        input_imag + lag_real,
        tables,
        ctx_count,
        radix_b,
        radix_c,
        channel_width,
    )
    final_scale = 1.0 / (2.0 * sequence_length * math.sqrt(sequence_length))
    return ((joint_real * final_scale).astype(jnp.bfloat16), joint_imag * final_scale)


def shards(proj, short_filter, long_filter, out_grad, conv_out):
    ctx_count = lax.axis_size("ctx")
    local_rows, local_channels = long_filter.shape
    tap_count = short_filter.shape[1]
    channel_width = local_channels // ctx_count
    sequence_length = local_rows * ctx_count
    norm_scale = float(sequence_length) ** (-0.5)
    arrived = (
        lax.all_to_all(
            to_pairs(proj[0], ctx_count), "ctx", split_axis=1, concat_axis=0, tiled=True
        ),
        lax.all_to_all(
            to_pairs(proj[1], ctx_count), "ctx", split_axis=1, concat_axis=0, tiled=True
        ),
        lax.all_to_all(
            to_pairs(proj[2], ctx_count), "ctx", split_axis=1, concat_axis=0, tiled=True
        ),
        lax.all_to_all(
            to_pairs(long_filter, ctx_count), "ctx", split_axis=1, concat_axis=0, tiled=True
        ),
        lax.all_to_all(
            to_pairs(out_grad, ctx_count), "ctx", split_axis=1, concat_axis=0, tiled=True
        ),
        lax.all_to_all(
            to_pairs(conv_out, ctx_count), "ctx", split_axis=1, concat_axis=0, tiled=True
        ),
    )
    streams = [
        arrived[0].astype(jnp.float32),
        arrived[1].astype(jnp.float32),
        arrived[2].astype(jnp.float32),
    ]
    filter_pairs = arrived[3]
    grad_pairs = arrived[4].astype(jnp.float32)
    saved_pairs = arrived[5].astype(jnp.float32)
    local_taps = lax.dynamic_slice_in_dim(
        short_filter, lax.axis_index("ctx") * channel_width, channel_width, 2
    )
    local_taps = jnp.concatenate([local_taps, local_taps], axis=2)
    delayed = [
        [retard(streams[stream], offset, channel_width) for offset in range(tap_count)]
        for stream in range(3)
    ]
    mixed = []
    for stream in range(3):
        running = local_taps[stream, 0][None, :] * delayed[stream][0]
        for offset in range(1, tap_count):
            running = running + local_taps[stream, offset][None, :] * delayed[stream][offset]
        mixed.append(running)
    product_u = (mixed[1] * mixed[2]).astype(jnp.bfloat16)
    product_g = (grad_pairs * mixed[0]).astype(jnp.bfloat16)
    input_pairs, lag_pairs = spectral(filter_pairs, product_u, product_g, ctx_count, local_rows)
    input_values = input_pairs.astype(jnp.float32)
    stream_grads = [grad_pairs * saved_pairs, input_values * mixed[2], input_values * mixed[1]]
    outgoing = []
    tap_sums = []
    for stream in range(3):
        running = local_taps[stream, 0][None, :] * stream_grads[stream]
        for offset in range(1, tap_count):
            running = running + local_taps[stream, offset][None, :] * advance(
                stream_grads[stream], offset, channel_width
            )
        outgoing.append(running.astype(jnp.bfloat16))
        column_sums = []
        for offset in range(tap_count):
            column_total = jnp.sum(stream_grads[stream] * delayed[stream][offset], axis=0)
            column_sums.append(column_total[:channel_width] + column_total[channel_width:])
        tap_sums.append(jnp.stack(column_sums))
    returned = (
        lax.all_to_all(outgoing[0], "ctx", split_axis=0, concat_axis=1, tiled=True),
        lax.all_to_all(outgoing[1], "ctx", split_axis=0, concat_axis=1, tiled=True),
        lax.all_to_all(outgoing[2], "ctx", split_axis=0, concat_axis=1, tiled=True),
    )
    proj_grad = jnp.stack(
        [
            from_pairs(returned[0], ctx_count),
            from_pairs(returned[1], ctx_count),
            from_pairs(returned[2], ctx_count),
        ]
    )
    short_grad = lax.all_gather(jnp.stack(tap_sums), "ctx", axis=2, tiled=True) * norm_scale
    filter_grad = from_pairs(
        lax.all_to_all(lag_pairs, "ctx", split_axis=0, concat_axis=1, tiled=True), ctx_count
    )
    square_total = lax.psum(jnp.sum(filter_grad * filter_grad), ("ctx", "ch"))
    grad_square = square_total / float(sequence_length * local_channels * lax.axis_size("ch"))
    return (proj_grad, short_grad, filter_grad, grad_square)


LANES = 128
HALO = 8
MESH = pl.DeviceIdType.MESH
H, G, U, DU, LAG, PART, FINAL, SQUARE = range(8)


def real_tables(length):
    period = 2 * length
    k = np.arange(length, dtype=np.int64)[:, None]
    t = np.arange(length, dtype=np.int64)[None, :]
    angle = (k * t % period) * (2.0 * np.pi / period)
    sine = np.sin(angle)
    sine[0] = 1.0 - 2.0 * (np.arange(length) % 2)
    table = np.concatenate([np.cos(angle), sine], axis=0)
    return table.astype(ml_dtypes.bfloat16), np.ascontiguousarray(table.T).astype(ml_dtypes.bfloat16)


def fused_kernel(
    n,
    heads,
    proj,
    taps,
    long_filter,
    out_grad,
    conv_out,
    table_hbm,
    inverse_hbm,
    proj_grad,
    short_grad,
    filter_grad,
    square,
    table,
    inverse,
    halo_down,
    halo_up,
    from_prev,
    from_next,
    ext,
    mixed,
    gate,
    send_g,
    send_u,
    got_h,
    got_g,
    got_u,
    spectrum,
    product,
    du_all,
    lag_all,
    got_du,
    got_lag,
    part,
    got_part,
    final,
    got_final,
    total_ctx,
    got_ctx,
    total_ch,
    got_ch,
    send_sem,
    recv_sem,
    halo_sem,
    head_sem,
    table_sem,
):
    me = lax.axis_index("ctx")
    head = lax.axis_index("ch")
    rows = long_filter.shape[0]
    length = n * rows
    taps_count = taps.shape[1]
    norm = float(length) ** -0.5
    prev, following = lax.rem(me + n - 1, n), lax.rem(me + 1, n)

    def lanes(index):
        return pl.ds(pl.multiple_of(index * LANES, LANES), LANES)

    def block(index, size=rows):
        return pl.ds(pl.multiple_of(index * rows, rows), size)

    def send(kind, peer, source, target):
        return pltpu.make_async_remote_copy(
            src_ref=source,
            dst_ref=target,
            send_sem=send_sem.at[kind, peer],
            recv_sem=recv_sem.at[kind, me],
            device_id=(peer, head),
            device_id_type=MESH,
        )

    def arrive(kind, peer, target):
        pltpu.make_async_remote_copy(
            src_ref=target,
            dst_ref=target,
            send_sem=send_sem.at[kind, peer],
            recv_sem=recv_sem.at[kind, peer],
            device_id=(peer, head),
            device_id_type=MESH,
        ).wait_recv()

    def peers(body):
        def step(i, carry):
            body(lax.rem(me + i, n))
            return carry

        lax.fori_loop(1, n, step, 0)

    barrier = pltpu.get_barrier_semaphore()
    for i in range(1, n):
        pl.semaphore_signal(
            barrier, inc=1, device_id=(lax.rem(me + i, n), head), device_id_type=MESH
        )
    for i in range(1, heads):
        pl.semaphore_signal(
            barrier, inc=1, device_id=(me, lax.rem(head + i, heads)), device_id_type=MESH
        )
    load_table = pltpu.make_async_copy(table_hbm, table, table_sem.at[0])
    load_inverse = pltpu.make_async_copy(inverse_hbm, inverse, table_sem.at[1])
    load_table.start()
    load_inverse.start()

    row = lax.broadcasted_iota(jnp.int32, (16, proj.shape[2]), 0)

    def pack(parts):
        packed = jnp.zeros(row.shape, jnp.float32)
        for place, (values, first) in enumerate(parts):
            shift = (2 * place - first) % 16
            moved = pltpu.roll(values.astype(jnp.float32), shift, 0) if shift else values.astype(jnp.float32)
            packed = jnp.where((row >= 2 * place) & (row < 2 * place + 2), moved, packed)
        return packed.astype(jnp.bfloat16)

    halo_down[...] = pack([(proj[j, rows - 16 : rows, :], 14) for j in range(3)])
    halo_up[...] = pack(
        [(proj[j, 0:16, :], 0) for j in range(3)] + [(out_grad[0:16, :], 0), (conv_out[0:16, :], 0)]
    )
    pl.semaphore_wait(barrier, n - 1 + heads - 1)

    def halo(source, target, index, peer):
        return pltpu.make_async_remote_copy(
            src_ref=source,
            dst_ref=target,
            send_sem=halo_sem.at[0, index],
            recv_sem=halo_sem.at[1, index],
            device_id=(peer, head),
            device_id_type=MESH,
        )

    down = halo(halo_down, from_prev, 0, following)
    up = halo(halo_up, from_next, 1, prev)
    down.start()
    up.start()

    def send_filter(peer):
        return send(H, peer, long_filter.at[:, lanes(peer)], got_h.at[block(me), :])

    peers(lambda peer: send_filter(peer).start())
    got_h[block(me), :] = long_filter[:, lanes(me)]
    part[...] = jnp.zeros_like(part)
    du_all[length : length + 16, :] = jnp.zeros((16, LANES), jnp.bfloat16)
    for j in range(3):
        ext[j, HALO : HALO + rows, :] = proj[j].astype(jnp.float32)
    ext[3, 0:rows, :] = out_grad[...].astype(jnp.float32) * conv_out[...].astype(jnp.float32)

    down.wait_recv()
    up.wait_recv()
    before = jnp.where(me == 0, 0.0, from_prev[...].astype(jnp.float32))
    after = jnp.where(me == n - 1, 0.0, from_next[...].astype(jnp.float32))
    for j in range(3):
        ext[j, 0:HALO, :] = pltpu.roll(before, (6 - 2 * j) % 16, 0)[0:8, :]
        ext[j, HALO + rows : 2 * HALO + rows, :] = (pltpu.roll(after, 16 - 2 * j, 0) if j else after)[0:8, :]
    ext[3, rows : rows + HALO, :] = (
        pltpu.roll(after, 10, 0)[0:8, :] * pltpu.roll(after, 8, 0)[0:8, :]
    )

    def gates(peer):
        at = lanes(peer)
        values = []
        for j in range(3):
            running = taps[j, 0:1, at] * ext[j, HALO : 2 * HALO + rows, at]
            for m in range(1, taps_count):
                running = running + taps[j, m : m + 1, at] * ext[j, HALO - m : 2 * HALO + rows - m, at]
            values.append(running)
        mixed[0, :, at] = values[1]
        mixed[1, :, at] = values[2]
        u = (values[1][:rows] * values[2][:rows]).astype(jnp.bfloat16)
        g = (out_grad[:, at].astype(jnp.float32) * values[0][:rows]).astype(jnp.bfloat16)
        return g, u

    def send_grad(peer):
        return send(G, peer, send_g.at[peer], got_g.at[block(me), :])

    def send_input(peer):
        return send(U, peer, send_u.at[peer], got_u.at[block(me), :])

    def gate_peer(peer):
        g, u = gates(peer)
        send_g[peer] = g
        send_u[peer] = u
        send_grad(peer).start()

    peers(gate_peer)
    peers(lambda peer: send_input(peer).start())
    g, u = gates(me)
    got_g[block(me), :] = g
    got_u[block(me), :] = u

    def stream(j, at, index, read):
        running = taps[j, 0:1, at] * read(0)
        for m in range(1, taps_count):
            running = running + taps[j, m : m + 1, at] * read(m)
        proj_grad[j, :, at] = running.astype(jnp.bfloat16)
        for m in range(taps_count):
            part[index, j * taps_count + m : j * taps_count + m + 1, :] = jnp.sum(
                read(0) * ext[j, HALO - m : HALO + rows - m, at], axis=0, keepdims=True
            )

    def first_stream(index, carry):
        at = lanes(index)
        stream(0, at, index, lambda m: ext[3, m : m + rows, at])
        return carry

    lax.fori_loop(0, n, first_stream, 0)

    step_rows = min(256, length)

    def transform(slot, source):
        def tile(i, carry):
            at = pl.ds(pl.multiple_of(i * step_rows, step_rows), step_rows)
            spectrum[slot, at, :] = jnp.dot(
                table[at, :], source[...], preferred_element_type=jnp.float32
            )
            return carry

        lax.fori_loop(0, 2 * length // step_rows, tile, 0)

    def correlate(slot):
        def tile(i, carry):
            low = pl.ds(pl.multiple_of(i * step_rows, step_rows), step_rows)
            high = pl.ds(pl.multiple_of(length + i * step_rows, step_rows), step_rows)
            a_cos, a_sin = spectrum[slot, low, :], spectrum[slot, high, :]
            g_cos, g_sin = spectrum[1, low, :], spectrum[1, high, :]
            edge = lax.broadcasted_iota(jnp.int32, (step_rows, LANES), 0) + i * step_rows == 0
            cos_cos, sin_sin = a_cos * g_cos, a_sin * g_sin
            product[low, :] = jnp.where(edge, 0.5 * cos_cos, cos_cos + sin_sin).astype(jnp.bfloat16)
            product[high, :] = jnp.where(
                edge, 0.5 * sin_sin, a_cos * g_sin - a_sin * g_cos
            ).astype(jnp.bfloat16)
            return carry

        lax.fori_loop(0, length // step_rows, tile, 0)

    def invert(store, start):
        def tile(i, carry):
            at = pl.ds(pl.multiple_of(i * step_rows, step_rows), step_rows)
            values = jnp.dot(inverse[at, :], product[...], preferred_element_type=jnp.float32)
            return store(at, values * (norm / length), carry)

        return lax.fori_loop(0, length // step_rows, tile, start)

    load_table.wait()
    peers(lambda peer: arrive(H, peer, got_h.at[block(peer), :]))
    transform(0, got_h)
    peers(lambda peer: arrive(G, peer, got_g.at[block(peer), :]))
    transform(1, got_g)
    correlate(0)
    load_inverse.wait()

    def store_du(at, values, carry):
        du_all[at, :] = values.astype(jnp.bfloat16)
        return carry

    invert(store_du, 0)

    def send_du(peer):
        return send(DU, peer, du_all.at[block(peer, rows + 16), :], got_du.at[me])

    peers(lambda peer: send_du(peer).start())
    got_du[me] = du_all[block(me, rows + 16), :]

    peers(lambda peer: arrive(U, peer, got_u.at[block(peer), :]))
    transform(2, got_u)
    correlate(2)

    def store_lag(at, values, carry):
        lag_all[at, :] = values.astype(jnp.bfloat16)
        return carry + jnp.sum((values * values).reshape(step_rows // 8, 8, LANES), axis=0)

    total_ctx[...] = invert(store_lag, jnp.zeros((8, LANES), jnp.float32))

    def send_square(peer):
        return send(SQUARE, peer, total_ctx, got_ctx.at[me])

    def send_lag(peer):
        return send(LAG, peer, lag_all.at[block(peer), :], got_lag.at[me])

    peers(lambda peer: send_square(peer).start())
    peers(lambda peer: send_lag(peer).start())

    def send_part(peer):
        return send(PART, peer, part.at[peer], got_part.at[me])

    def rest(index):
        at = lanes(index)
        du = got_du[index].astype(jnp.float32)[: rows + HALO]
        gate[0] = du * mixed[1, :, at]
        gate[1] = du * mixed[0, :, at]
        stream(1, at, index, lambda m: gate[0, m : m + rows, :])
        stream(2, at, index, lambda m: gate[1, m : m + rows, :])

    def rest_peer(peer):
        arrive(DU, peer, got_du.at[peer])
        rest(peer)
        send_part(peer).start()

    rest(me)
    peers(rest_peer)

    total = total_ctx[...]
    for i in range(1, n):
        peer = lax.rem(me + i, n)
        arrive(SQUARE, peer, got_ctx.at[peer])
        total = total + got_ctx[peer]
    total_ch[...] = total

    def send_head(i):
        return pltpu.make_async_remote_copy(
            src_ref=total_ch,
            dst_ref=got_ch.at[i],
            send_sem=head_sem.at[0, i],
            recv_sem=head_sem.at[1, i],
            device_id=(me, lax.rem(head + i, heads)),
            device_id_type=MESH,
        )

    for i in range(1, heads):
        send_head(i).start()

    sums = part[me]
    for i in range(1, n):
        peer = lax.rem(me + i, n)
        arrive(PART, peer, got_part.at[peer])
        sums = sums + got_part[peer]
    final[...] = sums * norm
    got_final[me] = sums * norm

    def send_final(peer):
        return send(FINAL, peer, final, got_final.at[me])

    peers(lambda peer: send_final(peer).start())

    filter_grad[:, lanes(me)] = lag_all[block(me), :].astype(jnp.float32)

    def take_lag(peer):
        arrive(LAG, peer, got_lag.at[peer])
        filter_grad[:, lanes(peer)] = got_lag[peer].astype(jnp.float32)

    peers(take_lag)

    total = total_ch[...]
    for i in range(1, heads):
        send_head(i).wait_recv()
        total = total + got_ch[i]
    square[...] = jnp.broadcast_to(
        jnp.sum(total, keepdims=True) / float(length * n * LANES * heads), square.shape
    )

    def put_final(index):
        at = lanes(index)
        for j in range(3):
            for m in range(taps_count):
                place = j * taps_count + m
                short_grad[j, m : m + 1, at] = got_final[index, place : place + 1, :]

    def take_final(peer):
        arrive(FINAL, peer, got_final.at[peer])
        put_final(peer)

    put_final(me)
    peers(take_final)

    down.wait_send()
    up.wait_send()
    for i in range(1, heads):
        send_head(i).wait_send()

    def sent(peer):
        for one in (
            send_filter,
            send_grad,
            send_input,
            send_du,
            send_square,
            send_lag,
            send_part,
            send_final,
        ):
            one(peer).wait_send()

    peers(sent)


def fused_shards(tables, proj, short_filter, long_filter, out_grad, conv_out):
    n = lax.axis_size("ctx")
    heads = lax.axis_size("ch")
    rows, channels = long_filter.shape
    length = n * rows
    bf16, f32 = jnp.bfloat16, jnp.float32
    vmem = pl.BlockSpec(memory_space=pltpu.VMEM)
    anywhere = pl.BlockSpec(memory_space=pl.ANY)
    outs = pl.pallas_call(
        functools.partial(fused_kernel, n, heads),
        out_shape=(
            jax.ShapeDtypeStruct((3, rows, channels), bf16),
            jax.ShapeDtypeStruct(short_filter.shape, f32),
            jax.ShapeDtypeStruct((rows, channels), f32),
            jax.ShapeDtypeStruct((8, LANES), f32),
        ),
        in_specs=[vmem] * 5 + [anywhere] * 2,
        out_specs=(vmem,) * 4,
        scratch_shapes=[
            pltpu.VMEM((2 * length, length), bf16),
            pltpu.VMEM((length, 2 * length), bf16),
            pltpu.VMEM((16, channels), bf16),
            pltpu.VMEM((16, channels), bf16),
            pltpu.VMEM((16, channels), bf16),
            pltpu.VMEM((16, channels), bf16),
            pltpu.VMEM((4, rows + 2 * HALO, channels), f32),
            pltpu.VMEM((2, rows + HALO, channels), f32),
            pltpu.VMEM((2, rows + HALO, LANES), f32),
            pltpu.VMEM((n, rows, LANES), bf16),
            pltpu.VMEM((n, rows, LANES), bf16),
            pltpu.VMEM((length, LANES), bf16),
            pltpu.VMEM((length, LANES), bf16),
            pltpu.VMEM((length, LANES), bf16),
            pltpu.VMEM((3, 2 * length, LANES), f32),
            pltpu.VMEM((2 * length, LANES), bf16),
            pltpu.VMEM((length + 16, LANES), bf16),
            pltpu.VMEM((length, LANES), bf16),
            pltpu.VMEM((n, rows + 16, LANES), bf16),
            pltpu.VMEM((n, rows, LANES), bf16),
            pltpu.VMEM((n, 16, LANES), f32),
            pltpu.VMEM((n, 16, LANES), f32),
            pltpu.VMEM((16, LANES), f32),
            pltpu.VMEM((n, 16, LANES), f32),
            pltpu.VMEM((8, LANES), f32),
            pltpu.VMEM((n, 8, LANES), f32),
            pltpu.VMEM((8, LANES), f32),
            pltpu.VMEM((heads, 8, LANES), f32),
            pltpu.SemaphoreType.DMA((8, n)),
            pltpu.SemaphoreType.DMA((8, n)),
            pltpu.SemaphoreType.DMA((2, 2)),
            pltpu.SemaphoreType.DMA((2, heads)),
            pltpu.SemaphoreType.DMA((2,)),
        ],
        compiler_params=pltpu.CompilerParams(
            collective_id=0, has_side_effects=True, vmem_limit_bytes=40 * 1024 * 1024
        ),
    )(proj, short_filter, long_filter, out_grad, conv_out, *tables)
    return (outs[0], outs[1], outs[2], outs[3][0, 0])


def program(proj, short_filter, long_filter, out_grad, conv_out):
    n = lax.axis_size("ctx")
    rows, channels = long_filter.shape
    length = n * rows
    fits = (
        channels == n * LANES
        and length in (256, 512, 1024)
        and rows % 16 == 0
        and n > 2
        and short_filter.shape[1] == 3
    )
    if not fits:
        return shards(proj, short_filter, long_filter, out_grad, conv_out)
    tables = [jnp.asarray(one) for one in real_tables(length)]
    return fused_shards(tables, proj, short_filter, long_filter, out_grad, conv_out)


def solution(mesh):
    return jax.shard_map(
        program,
        mesh=mesh,
        in_specs=(
            P(None, "ctx", "ch"),
            P(None, None, "ch"),
            P("ctx", "ch"),
            P("ctx", "ch"),
            P("ctx", "ch"),
        ),
        out_specs=(P(None, "ctx", "ch"), P(None, None, "ch"), P("ctx", "ch"), P()),
        check_vma=False,
    )
```

profile of v0, /device:TPU:0, one launch (start us, length us, event | category | flops | bytes accessed | tf_op | source)
XLA Modules:
  0.0 59.6 jit_solution(10354505310814756888)
XLA Ops:
  0.6 0.0 copy-start
  0.6 2.2 %copy-done = bf16[1024,2048]{1,0:T(8,128)(2,1)S(1)} copy-done((bf16[1024,2048]{1,0:T(8,128)(2,1)S(1)}, bf16[1024,2048]{1,0:T(8,128)(2,1)}, u32[]{:S(2)}) %copy-start) | copy-done | bytes 4194328
  2.8 0.0 copy-start.1
  2.8 2.2 %copy-done.1 = bf16[2048,1024]{1,0:T(8,128)(2,1)S(1)} copy-done((bf16[2048,1024]{1,0:T(8,128)(2,1)S(1)}, bf16[2048,1024]{1,0:T(8,128)(2,1)}, u32[]{:S(2)}) %copy-start.1) | copy-done | bytes 4194328
  5.0 0.0 copy-start.2
  5.0 1.1 %copy-done.2 = bf16[3,128,1024]{2,1,0:T(8,128)(2,1)S(1)} copy-done((bf16[3,128,1024]{2,1,0:T(8,128)(2,1)S(1)}, bf16[3,128,1024]{2,1,0:T(8,128)(2,1)}, u32[]{:S(2)}) %copy-start.2) | copy-done | bytes 786456
  6.1 0.0 copy-start.3
  6.1 0.9 %copy-done.3 = bf16[128,1024]{1,0:T(8,128)(2,1)S(1)} copy-done((bf16[128,1024]{1,0:T(8,128)(2,1)S(1)}, bf16[128,1024]{1,0:T(8,128)(2,1)}, u32[]{:S(2)}) %copy-start.3) | copy-done | bytes 262168
  7.1 0.0 copy-start.4
  7.1 0.9 %copy-done.4 = bf16[128,1024]{1,0:T(8,128)(2,1)S(1)} copy-done((bf16[128,1024]{1,0:T(8,128)(2,1)S(1)}, bf16[128,1024]{1,0:T(8,128)(2,1)}, u32[]{:S(2)}) %copy-start.4) | copy-done | bytes 262168
  8.0 0.0 copy-start.5
  8.0 0.9 %copy-done.5 = bf16[128,1024]{1,0:T(8,128)(2,1)S(1)} copy-done((bf16[128,1024]{1,0:T(8,128)(2,1)S(1)}, bf16[128,1024]{1,0:T(8,128)(2,1)}, u32[]{:S(2)}) %copy-start.5) | copy-done | bytes 262168
  9.0 0.0 copy-start.6
  9.0 0.8 %copy-done.6 = f32[3,3,1024]{2,1,0:T(4,128)S(1)} copy-done((f32[3,3,1024]{2,1,0:T(4,128)S(1)}, f32[3,3,1024]{2,1,0:T(4,128)}, u32[]{:S(2)}) %copy-start.6) | copy-done | bytes 36888
  9.8 46.9 %shard_map.102 = (bf16[3,128,1024]{2,1,0:T(8,128)(2,1)S(1)}, f32[3,3,1024]{2,1,0:T(4,128)S(1)}, f32[128,1024]{1,0:T(8,128)S(1)}, f32[8,128]{1,0:T(8,128)S(1)}) custom-call(bf16[3,128,1024]{2,1,0:T(8,128)(2,1)S(1)} %copy-done.2, f32[3,3,1024]{2,1,0:T(4,128)S(1)} %copy-done.6, bf16[128,1024]{1,0:T(8,128)(2,1)S(1)} %copy-done.3, ...), custom_call_target="tpu_custom_call" | custom-call | tf_op jit(solution)/shard_map/pallas_call | solution.py:689
  56.8 0.5 slice.3
  57.3 0.9 %copy.14 = bf16[3,128,1024]{2,1,0:T(8,128)(2,1)} copy(bf16[3,128,1024]{2,1,0:T(8,128)(2,1)S(1)} %get-tuple-element.16) | data formatting | bytes 1572864
  58.1 0.6 %copy.15 = f32[3,3,1024]{2,1,0:T(4,128)} copy(f32[3,3,1024]{2,1,0:T(4,128)S(1)} %get-tuple-element.17) | data formatting | bytes 73728
  58.8 0.8 %copy.16 = f32[128,1024]{1,0:T(8,128)} copy(f32[128,1024]{1,0:T(8,128)S(1)} %get-tuple-element.18) | data formatting | bytes 1048576
Async XLA Ops:
  0.6 2.2 %copy-start = (bf16[1024,2048]{1,0:T(8,128)(2,1)S(1)}, bf16[1024,2048]{1,0:T(8,128)(2,1)}, u32[]{:S(2)}) copy-start(bf16[1024,2048]{1,0:T(8,128)(2,1)} %constant.5.clone.inverse_hbm) | copy-start | bytes 12582916
  2.8 2.2 %copy-start.1 = (bf16[2048,1024]{1,0:T(8,128)(2,1)S(1)}, bf16[2048,1024]{1,0:T(8,128)(2,1)}, u32[]{:S(2)}) copy-start(bf16[2048,1024]{1,0:T(8,128)(2,1)} %constant.4.clone.table_hbm) | copy-start | bytes 12582916
  5.0 1.1 %copy-start.2 = (bf16[3,128,1024]{2,1,0:T(8,128)(2,1)S(1)}, bf16[3,128,1024]{2,1,0:T(8,128)(2,1)}, u32[]{:S(2)}) copy-start(bf16[3,128,1024]{2,1,0:T(8,128)(2,1)} %proj.1) | copy-start | bytes 2359300
  6.1 0.9 %copy-start.3 = (bf16[128,1024]{1,0:T(8,128)(2,1)S(1)}, bf16[128,1024]{1,0:T(8,128)(2,1)}, u32[]{:S(2)}) copy-start(bf16[128,1024]{1,0:T(8,128)(2,1)} %long_filter.1) | copy-start | bytes 786436
  7.1 0.9 %copy-start.4 = (bf16[128,1024]{1,0:T(8,128)(2,1)S(1)}, bf16[128,1024]{1,0:T(8,128)(2,1)}, u32[]{:S(2)}) copy-start(bf16[128,1024]{1,0:T(8,128)(2,1)} %out_grad.1) | copy-start | bytes 786436
  8.0 0.9 %copy-start.5 = (bf16[128,1024]{1,0:T(8,128)(2,1)S(1)}, bf16[128,1024]{1,0:T(8,128)(2,1)}, u32[]{:S(2)}) copy-start(bf16[128,1024]{1,0:T(8,128)(2,1)} %conv_out.1) | copy-start | bytes 786436
  9.0 0.8 %copy-start.6 = (f32[3,3,1024]{2,1,0:T(4,128)S(1)}, f32[3,3,1024]{2,1,0:T(4,128)}, u32[]{:S(2)}) copy-start(f32[3,3,1024]{2,1,0:T(4,128)} %taps.1) | copy-start | bytes 110596
where the time goes:
time: 59.9 us; the launch traced here: 59.6 us
  Pallas kernels  46.9 us (78%)
  local copies, waits for them, and re-layouts  12 us (20%)
  between operations  0.66 us (1%)
    pallas_call x1, Pallas kernels, fused_shards(): pl.pallas_call(functools.partial(fused_kernel, n, heads), out_shape=(jax....  46.9 us
    unnamed x17, local copies, waits for them, and re-layouts  11.4 us

commit v1 on v0

--- a/solution.py
+++ b/solution.py
@@ -298,17 +298,21 @@
 def fused_kernel(
     n,
     heads,
-    proj,
-    taps,
+    proj_hbm,
+    taps_hbm,
     long_filter,
-    out_grad,
-    conv_out,
+    out_grad_hbm,
+    conv_out_hbm,
     table_hbm,
     inverse_hbm,
     proj_grad,
     short_grad,
     filter_grad,
     square,
+    proj,
+    taps,
+    out_grad,
+    conv_out,
     table,
     inverse,
     halo_down,
@@ -384,6 +388,21 @@
 
         lax.fori_loop(1, n, step, 0)
 
+    load_table = pltpu.make_async_copy(table_hbm, table, table_sem.at[0])
+    load_inverse = pltpu.make_async_copy(inverse_hbm, inverse, table_sem.at[1])
+    loads = [
+        pltpu.make_async_copy(proj_hbm, proj, table_sem.at[2]),
+        pltpu.make_async_copy(out_grad_hbm, out_grad, table_sem.at[3]),
+        pltpu.make_async_copy(conv_out_hbm, conv_out, table_sem.at[4]),
+        pltpu.make_async_copy(taps_hbm, taps, table_sem.at[5]),
+    ]
+    for load in loads:
+        load.start()
+    own_filter = pltpu.make_async_copy(
+        long_filter.at[:, lanes(me)], got_h.at[block(me), :], table_sem.at[6]
+    )
+    own_filter.start()
+
     barrier = pltpu.get_barrier_semaphore()
     for i in range(1, n):
         pl.semaphore_signal(
@@ -393,11 +412,11 @@
         pl.semaphore_signal(
             barrier, inc=1, device_id=(me, lax.rem(head + i, heads)), device_id_type=MESH
         )
-    load_table = pltpu.make_async_copy(table_hbm, table, table_sem.at[0])
-    load_inverse = pltpu.make_async_copy(inverse_hbm, inverse, table_sem.at[1])
+
+    for load in loads:
+        load.wait()
     load_table.start()
     load_inverse.start()
-
     row = lax.broadcasted_iota(jnp.int32, (16, proj.shape[2]), 0)
 
     def pack(parts):
@@ -433,7 +452,6 @@
         return send(H, peer, long_filter.at[:, lanes(peer)], got_h.at[block(me), :])
 
     peers(lambda peer: send_filter(peer).start())
-    got_h[block(me), :] = long_filter[:, lanes(me)]
     part[...] = jnp.zeros_like(part)
     du_all[length : length + 16, :] = jnp.zeros((16, LANES), jnp.bfloat16)
     for j in range(3):
@@ -500,7 +518,7 @@
 
     lax.fori_loop(0, n, first_stream, 0)
 
-    step_rows = min(256, length)
+    step_rows = min(1024, length)
 
     def transform(slot, source):
         def tile(i, carry):
@@ -537,6 +555,7 @@
         return lax.fori_loop(0, length // step_rows, tile, start)
 
     load_table.wait()
+    own_filter.wait()
     peers(lambda peer: arrive(H, peer, got_h.at[block(peer), :]))
     transform(0, got_h)
     peers(lambda peer: arrive(G, peer, got_g.at[block(peer), :]))
@@ -685,18 +704,22 @@
     length = n * rows
     bf16, f32 = jnp.bfloat16, jnp.float32
     vmem = pl.BlockSpec(memory_space=pltpu.VMEM)
-    anywhere = pl.BlockSpec(memory_space=pl.ANY)
+    hbm = pl.BlockSpec(memory_space=pltpu.HBM)
     outs = pl.pallas_call(
         functools.partial(fused_kernel, n, heads),
         out_shape=(
-            jax.ShapeDtypeStruct((3, rows, channels), bf16),
-            jax.ShapeDtypeStruct(short_filter.shape, f32),
-            jax.ShapeDtypeStruct((rows, channels), f32),
-            jax.ShapeDtypeStruct((8, LANES), f32),
-        ),
-        in_specs=[vmem] * 5 + [anywhere] * 2,
+            pltpu.VMEM((3, rows, channels), bf16),
+            pltpu.VMEM(short_filter.shape, f32),
+            pltpu.VMEM((rows, channels), f32),
+            pltpu.VMEM((8, LANES), f32),
+        ),
+        in_specs=[hbm] * 7,
         out_specs=(vmem,) * 4,
         scratch_shapes=[
+            pltpu.VMEM((3, rows, channels), bf16),
+            pltpu.VMEM(short_filter.shape, f32),
+            pltpu.VMEM((rows, channels), bf16),
+            pltpu.VMEM((rows, channels), bf16),
             pltpu.VMEM((2 * length, length), bf16),
             pltpu.VMEM((length, 2 * length), bf16),
             pltpu.VMEM((16, channels), bf16),
@@ -729,10 +752,10 @@
             pltpu.SemaphoreType.DMA((8, n)),
             pltpu.SemaphoreType.DMA((2, 2)),
             pltpu.SemaphoreType.DMA((2, heads)),
-            pltpu.SemaphoreType.DMA((2,)),
+            pltpu.SemaphoreType.DMA((7,)),
         ],
         compiler_params=pltpu.CompilerParams(
-            collective_id=0, has_side_effects=True, vmem_limit_bytes=40 * 1024 * 1024
+            collective_id=0, has_side_effects=True, vmem_limit_bytes=54 * 1024 * 1024
         ),
     )(proj, short_filter, long_filter, out_grad, conv_out, *tables)
     return (outs[0], outs[1], outs[2], outs[3][0, 0])

time: 59.9 us -> 48.9 us (0.82)
  local copies, waits for them, and re-layouts: 12 us -> 2.8 us
  Pallas kernels: 46.9 us -> 45.3 us
    unnamed x17 -> x3, local copies, waits for them, and re-layouts: 11.4 us -> 2.29 us
    pallas_call x1, Pallas kernels: 46.9 us -> 45.3 us  [fused_shards(): pl.pallas_call(functools.partial(fused_kernel, n, heads), out_shape=(pltp...]
where the time goes in v1:
time: 48.9 us; the launch traced here: 48.8 us
  Pallas kernels  45.3 us (93%)
  local copies, waits for them, and re-layouts  2.8 us (6%)
  between operations  0.64 us (1%)
    pallas_call x1, Pallas kernels, fused_shards(): pl.pallas_call(functools.partial(fused_kernel, n, heads), out_shape=(pltp...  45.3 us
    unnamed x3, local copies, waits for them, and re-layouts  2.29 us

profile of v1, /device:TPU:0, one launch (start us, length us, event | category | flops | bytes accessed | tf_op | source)
XLA Modules:
  0.0 48.8 jit_solution(11495421441769138096)
XLA Ops:
  0.6 45.3 %shard_map.102 = (bf16[3,128,1024]{2,1,0:T(8,128)(2,1)S(1)}, f32[3,3,1024]{2,1,0:T(4,128)S(1)}, f32[128,1024]{1,0:T(8,128)S(1)}, f32[8,128]{1,0:T(8,128)S(1)}) custom-call(bf16[3,128,1024]{2,1,0:T(8,128)(2,1)} %proj_hbm.1, f32[3,3,1024]{2,1,0:T(4,128)} %taps_hbm.1, bf16[128,1024]{1,0:T(8,128)(2,1)} %long_filter.1, bf16[128,1024]{1,0:T(8,128)(2,1)} %out_grad_hbm.1, ...), custom_call_target="tpu_custom_call" | custom-call | tf_op jit(solution)/shard_map/pallas_call | solution.py:708
  46.0 0.5 %slice.3 = f32[1,1]{1,0:T(1,128)} slice(f32[8,128]{1,0:T(8,128)S(1)} %get-tuple-element.11), slice={[0:1], [0:1]} | slice | bytes 8 | tf_op jit(solution)/shard_map/slice | solution.py:761
  46.5 0.9 %copy.14 = bf16[3,128,1024]{2,1,0:T(8,128)(2,1)} copy(bf16[3,128,1024]{2,1,0:T(8,128)(2,1)S(1)} %get-tuple-element.12) | data formatting | bytes 1572864
  47.4 0.6 %copy.15 = f32[3,3,1024]{2,1,0:T(4,128)} copy(f32[3,3,1024]{2,1,0:T(4,128)S(1)} %get-tuple-element.13) | data formatting | bytes 73728
  48.0 0.8 %copy.16 = f32[128,1024]{1,0:T(8,128)} copy(f32[128,1024]{1,0:T(8,128)S(1)} %get-tuple-element.14) | data formatting | bytes 1048576

commit v2 on v1

--- a/solution.py
+++ b/solution.py
@@ -281,7 +281,7 @@
 LANES = 128
 HALO = 8
 MESH = pl.DeviceIdType.MESH
-H, G, U, DU, LAG, PART, FINAL, SQUARE = range(8)
+H, G, U, DU, LAG, PART, FINAL = range(7)
 
 
 def real_tables(length):
@@ -334,11 +334,10 @@
     got_du,
     got_lag,
     part,
+    part_out,
     got_part,
     final,
     got_final,
-    total_ctx,
-    got_ctx,
     total_ch,
     got_ch,
     send_sem,
@@ -583,19 +582,17 @@
         lag_all[at, :] = values.astype(jnp.bfloat16)
         return carry + jnp.sum((values * values).reshape(step_rows // 8, 8, LANES), axis=0)
 
-    total_ctx[...] = invert(store_lag, jnp.zeros((8, LANES), jnp.float32))
-
-    def send_square(peer):
-        return send(SQUARE, peer, total_ctx, got_ctx.at[me])
+    own_square = invert(store_lag, jnp.zeros((8, LANES), jnp.float32))
 
     def send_lag(peer):
         return send(LAG, peer, lag_all.at[block(peer), :], got_lag.at[me])
 
-    peers(lambda peer: send_square(peer).start())
     peers(lambda peer: send_lag(peer).start())
 
     def send_part(peer):
-        return send(PART, peer, part.at[peer], got_part.at[me])
+        return send(PART, peer, part_out.at[peer], got_part.at[me])
+
+    square_row = jnp.sum(own_square, axis=0, keepdims=True)
 
     def rest(index):
         at = lanes(index)
@@ -604,6 +601,8 @@
         gate[1] = du * mixed[0, :, at]
         stream(1, at, index, lambda m: gate[0, m : m + rows, :])
         stream(2, at, index, lambda m: gate[1, m : m + rows, :])
+        part[index, 9:10, :] = square_row
+        part_out[index] = part[index].astype(jnp.bfloat16)
 
     def rest_peer(peer):
         arrive(DU, peer, got_du.at[peer])
@@ -613,12 +612,19 @@
     rest(me)
     peers(rest_peer)
 
-    total = total_ctx[...]
+    sums = part_out[me].astype(jnp.float32)
     for i in range(1, n):
         peer = lax.rem(me + i, n)
-        arrive(SQUARE, peer, got_ctx.at[peer])
-        total = total + got_ctx[peer]
-    total_ch[...] = total
+        arrive(PART, peer, got_part.at[peer])
+        sums = sums + got_part[peer].astype(jnp.float32)
+    final[...] = (sums * norm).astype(jnp.bfloat16)
+    got_final[me] = (sums * norm).astype(jnp.bfloat16)
+
+    def send_final(peer):
+        return send(FINAL, peer, final, got_final.at[me])
+
+    peers(lambda peer: send_final(peer).start())
+    total_ch[...] = jnp.broadcast_to(sums[9:10], total_ch.shape)
 
     def send_head(i):
         return pltpu.make_async_remote_copy(
@@ -633,19 +639,6 @@
     for i in range(1, heads):
         send_head(i).start()
 
-    sums = part[me]
-    for i in range(1, n):
-        peer = lax.rem(me + i, n)
-        arrive(PART, peer, got_part.at[peer])
-        sums = sums + got_part[peer]
-    final[...] = sums * norm
-    got_final[me] = sums * norm
-
-    def send_final(peer):
-        return send(FINAL, peer, final, got_final.at[me])
-
-    peers(lambda peer: send_final(peer).start())
-
     filter_grad[:, lanes(me)] = lag_all[block(me), :].astype(jnp.float32)
 
     def take_lag(peer):
@@ -659,15 +652,16 @@
         send_head(i).wait_recv()
         total = total + got_ch[i]
     square[...] = jnp.broadcast_to(
-        jnp.sum(total, keepdims=True) / float(length * n * LANES * heads), square.shape
+        jnp.sum(total[0:1], keepdims=True) / float(length * n * LANES * heads), square.shape
     )
 
     def put_final(index):
         at = lanes(index)
+        values = got_final[index].astype(jnp.float32)
         for j in range(3):
             for m in range(taps_count):
                 place = j * taps_count + m
-                short_grad[j, m : m + 1, at] = got_final[index, place : place + 1, :]
+                short_grad[j, m : m + 1, at] = values[place : place + 1]
 
     def take_final(peer):
         arrive(FINAL, peer, got_final.at[peer])
@@ -687,7 +681,6 @@
             send_grad,
             send_input,
             send_du,
-            send_square,
             send_lag,
             send_part,
             send_final,
@@ -741,15 +734,14 @@
             pltpu.VMEM((n, rows + 16, LANES), bf16),
             pltpu.VMEM((n, rows, LANES), bf16),
             pltpu.VMEM((n, 16, LANES), f32),
-            pltpu.VMEM((n, 16, LANES), f32),
-            pltpu.VMEM((16, LANES), f32),
-            pltpu.VMEM((n, 16, LANES), f32),
-            pltpu.VMEM((8, LANES), f32),
-            pltpu.VMEM((n, 8, LANES), f32),
+            pltpu.VMEM((n, 16, LANES), bf16),
+            pltpu.VMEM((n, 16, LANES), bf16),
+            pltpu.VMEM((16, LANES), bf16),
+            pltpu.VMEM((n, 16, LANES), bf16),
             pltpu.VMEM((8, LANES), f32),
             pltpu.VMEM((heads, 8, LANES), f32),
-            pltpu.SemaphoreType.DMA((8, n)),
-            pltpu.SemaphoreType.DMA((8, n)),
+            pltpu.SemaphoreType.DMA((7, n)),
+            pltpu.SemaphoreType.DMA((7, n)),
             pltpu.SemaphoreType.DMA((2, 2)),
             pltpu.SemaphoreType.DMA((2, heads)),
             pltpu.SemaphoreType.DMA((7,)),

time: 48.9 us -> 47.8 us (0.978)
  Pallas kernels: 45.3 us -> 44.3 us
    pallas_call x1, Pallas kernels: 45.3 us -> 44.3 us  [fused_shards(): pl.pallas_call(functools.partial(fused_kernel, n, heads), out_shape=(pltp...]
where the time goes in v2:
time: 47.8 us; the launch traced here: 47.7 us
  Pallas kernels  44.3 us (93%)
  local copies, waits for them, and re-layouts  2.8 us (6%)
  between operations  0.64 us (1%)
    pallas_call x1, Pallas kernels, fused_shards(): pl.pallas_call(functools.partial(fused_kernel, n, heads), out_shape=(pltp...  44.3 us
    unnamed x3, local copies, waits for them, and re-layouts  2.29 us

profile of v2, /device:TPU:0, one launch (start us, length us, event | category | flops | bytes accessed | tf_op | source)
XLA Modules:
  0.0 47.7 jit_solution(13106945038406516440)
XLA Ops:
  0.6 44.3 %shard_map.102 = (bf16[3,128,1024]{2,1,0:T(8,128)(2,1)S(1)}, f32[3,3,1024]{2,1,0:T(4,128)S(1)}, f32[128,1024]{1,0:T(8,128)S(1)}, f32[8,128]{1,0:T(8,128)S(1)}) custom-call(bf16[3,128,1024]{2,1,0:T(8,128)(2,1)} %proj_hbm.1, f32[3,3,1024]{2,1,0:T(4,128)} %taps_hbm.1, bf16[128,1024]{1,0:T(8,128)(2,1)} %long_filter.1, bf16[128,1024]{1,0:T(8,128)(2,1)} %out_grad_hbm.1, ...), custom_call_target="tpu_custom_call" | custom-call | tf_op jit(solution)/shard_map/pallas_call | solution.py:701
  44.9 0.5 %slice.3 = f32[1,1]{1,0:T(1,128)} slice(f32[8,128]{1,0:T(8,128)S(1)} %get-tuple-element.11), slice={[0:1], [0:1]} | slice | bytes 8 | tf_op jit(solution)/shard_map/slice | solution.py:753
  45.4 0.9 %copy.14 = bf16[3,128,1024]{2,1,0:T(8,128)(2,1)} copy(bf16[3,128,1024]{2,1,0:T(8,128)(2,1)S(1)} %get-tuple-element.12) | data formatting | bytes 1572864
  46.3 0.6 %copy.15 = f32[3,3,1024]{2,1,0:T(4,128)} copy(f32[3,3,1024]{2,1,0:T(4,128)S(1)} %get-tuple-element.13) | data formatting | bytes 73728
  46.9 0.8 %copy.16 = f32[128,1024]{1,0:T(8,128)} copy(f32[128,1024]{1,0:T(8,128)S(1)} %get-tuple-element.14) | data formatting | bytes 1048576
